TPU v7x, 512 devices: a whole 4x4x16 slice. The times are simulated.
512 devices in a mesh: dp: 8 (over x, core), expert: 64 (over y, z).
Axes of the slice: x: 4, y: 4, z: 16, core: 2. Of those that a mesh axis runs over, the one named last changes fastest.
Arguments:
- tokens_in: bfloat16 [65536, 3584], P(('dp', 'expert')), may hold values from -6 to 6
- out_grad: bfloat16 [65536, 3584], P(('dp', 'expert')), may hold values from -0.59765625 to 0.59765625
- router_logits: float32 [65536, 192], P(('dp', 'expert')), may hold values from -12 to 250
- expert_ids: int32 [65536, 8], P(('dp', 'expert')), may hold values from 0 to 191, all different within a row; in each aligned block of 128 rows (0 to 127, 128 to 255, ...) at most 8 rows name the same one
- saved_hidden: bfloat16 [8, 64, 64, 8, 1024], P('dp', 'expert'), may hold values from -6 to 6
- down_weight: bfloat16 [64, 1024, 3584], P('expert', 'dp'), may hold values from -0.1875 to 0.1875
Outputs:
- hidden_grad: bfloat16 [8, 64, 64, 8, 1024], P('dp', 'expert')
- logit_grad: float32 [65536, 192], P(('dp', 'expert'))
- router_grad: float32 [3584, 192], P('expert', 'dp')
Inputs may be any that keep to these rules, and one draw needn't show every extreme that they name: `expert_ids`: among the 128 rows of one device no expert is named by more than 8 rows, a bound that some block reaches.
All inputs are finite; a program needn't handle non-finite values.
Results may differ from a plain program's by a relative error of at most 0.013.
Values may be sent and summed in bfloat16 or wider, within the bound.
A program may use at most 64 MiB of HBM per device.

v0:
```python
import jax
import jax.numpy as jnp
from jax import lax
from jax.sharding import PartitionSpec as P

RSCALE = 2.827
ZLOSS = 0.25


def entering(shard, axis, combine, identity):
    length, place = (lax.axis_size(axis), lax.axis_index(axis))
    everything = lax.all_gather(shard.astype(jnp.bfloat16), axis)
    start = jnp.broadcast_to(jnp.asarray(identity, shard.dtype), shard.shape)

    def lap(k, before):
        reached = k < place
        new = combine(before, everything[k].astype(shard.dtype))
        return jnp.where(reached, new, before)

    return lax.fori_loop(0, length, lap, start)


def from_root(value, axis, source):
    kept = jnp.where(lax.axis_index(axis) == source, value, 0).astype(value.dtype)
    return lax.psum(kept, axis)


def slot_table(ids_block, flight, cap):
    owners = jnp.arange(flight, dtype=jnp.int32)
    chosen = jnp.any(ids_block[:, :, None] == owners[None, None, :], axis=1)
    as_int = chosen.astype(jnp.int32)
    rank = jnp.cumsum(as_int, axis=0) - as_int
    places = jnp.arange(cap, dtype=jnp.int32)
    table = chosen[None, :, :] & (rank[None, :, :] == places[:, None, None])
    return jnp.transpose(table, (2, 0, 1))


def own_columns(panel):
    count = panel.shape[1] // lax.axis_size("dp")
    return lax.dynamic_slice_in_dim(panel, lax.axis_index("dp") * count, count, 1)


def local(tokens_in, out_grad, router_logits, expert_ids, saved_hidden, down_weight):
    highest = lax.Precision.HIGHEST
    flight = lax.axis_size("expert")
    cap = saved_hidden.shape[3]
    hidden = saved_hidden.shape[4]
    width = out_grad.shape[1]
    experts = router_logits.shape[1]
    top = jnp.max(router_logits, axis=1, keepdims=True)
    shifted = jnp.exp(router_logits - top)
    total = jnp.sum(shifted, axis=1, keepdims=True)
    probs = shifted / total
    lse = top + jnp.log(total)
    columns = jnp.arange(experts, dtype=jnp.int32)
    picks = (expert_ids[:, :, None] == columns[None, None, :]).astype(jnp.float32)
    chosen_logit = jnp.sum(picks * router_logits[:, None, :], axis=2)
    scores = jax.nn.sigmoid(chosen_logit)
    ssum = jnp.sum(scores, axis=1, keepdims=True)
    gates = RSCALE * scores / ssum
    gate_half = gates.astype(jnp.bfloat16)
    in_window = picks[:, :, :flight]
    gate_te = jnp.sum(in_window * gate_half.astype(jnp.float32)[:, :, None], axis=1)
    table = slot_table(expert_ids, flight, cap)
    table_half = table.astype(jnp.bfloat16)
    table_full = table.astype(jnp.float32)
    send_rows = jnp.einsum(
        "ect,td->ecd", table_half, out_grad, preferred_element_type=jnp.float32
    ).astype(jnp.bfloat16)
    send_gates = jnp.einsum("ect,te->ec", table_full, gate_te, precision=highest).astype(
        jnp.bfloat16
    )
    recv_rows, recv_gates = (
        lax.all_to_all(send_rows, "expert", split_axis=0, concat_axis=0, tiled=True),
        lax.all_to_all(send_gates, "expert", split_axis=0, concat_axis=0, tiled=True),
    )
    flat_rows = recv_rows.reshape(flight * cap, width)
    part = lax.dot_general(
        flat_rows,
        lax.all_gather(down_weight, "dp", axis=1, tiled=True)[0],
        (((1,), (1,)), ((), ())),
        preferred_element_type=jnp.float32,
    )
    slot_gates = recv_gates.reshape(flight * cap, 1).astype(jnp.float32)
    hidden_grad = (slot_gates * part).astype(jnp.bfloat16).reshape(1, 1, flight, cap, hidden)
    saved_flat = saved_hidden.reshape(flight * cap, hidden)
    gate_grad = jnp.sum(saved_flat * part, axis=1).reshape(flight, cap)
    returned = lax.all_to_all(gate_grad, "expert", split_axis=0, concat_axis=0, tiled=True)
    grad_te = jnp.einsum("ect,ec->te", table_full, returned, precision=highest)
    grad_choice = jnp.sum(in_window * grad_te[:, None, :], axis=2)
    mixed = jnp.sum(grad_choice * gates, axis=1, keepdims=True) / RSCALE
    dscore = RSCALE / ssum * (grad_choice - mixed)
    dchosen = dscore * scores * (1.0 - scores)
    logit_grad = jnp.sum(picks * dchosen[:, :, None], axis=1) + 2.0 * ZLOSS * lse * probs
    tokens_full = tokens_in.astype(jnp.float32)
    own_rows = lax.psum_scatter(
        lax.dot_general(tokens_full, logit_grad, (((0,), (0,)), ((), ())), precision=highest),
        "expert",
        scatter_dimension=0,
        tiled=True,
    )
    before = entering(
        own_rows, "dp", lambda earlier, later: earlier + later, jnp.zeros_like(own_rows)
    )
    finished = before + own_rows
    spread = from_root(finished.astype(jnp.bfloat16), "dp", lax.axis_size("dp") - 1).astype(
        finished.dtype
    )
    router_grad = own_columns(spread)
    return (hidden_grad, logit_grad, router_grad)


def solution(mesh):
    in_specs = (
        P(("dp", "expert"), None),
        P(("dp", "expert"), None),
        P(("dp", "expert"), None),
        P(("dp", "expert"), None),
        P("dp", "expert", None, None, None),
        P("expert", "dp", None),
    )
    out_specs = (P("dp", "expert", None, None, None), P(("dp", "expert"), None), P("expert", "dp"))
    return jax.shard_map(local, mesh=mesh, in_specs=in_specs, out_specs=out_specs, check_vma=False)
```

profile of v0, /device:TPU:1, one launch (start us, length us, event | category | flops | bytes accessed | tf_op | source)
XLA Modules:
  0.0 973.6 jit_solution(7703707765535747499)
XLA Ops:
  7.2 0.8 fusion.6
  8.5 3.0 convolution_convert_fusion
  11.5 19.6 %all-to-all-start.1 = ((bf16[64,8,3584]{2,1,0:T(8,128)(2,1)}), bf16[64,8,3584]{2,1,0:T(8,128)(2,1)}, u32[]{:S(2)}, u32[]{:S(2)}) async-start(bf16[64,8,3584]{2,1,0:T(8,128)(2,1)} %convolution_convert_fusion), calls=%async_computation.1 | async-start | bytes 7340032 | tf_op jit(solution)/shard_map/all_to_all | solution.py:74
  31.2 0.7 all-gather.3.cloned.1.call-update
  32.3 56.4 %all-gather.3.cloned.1.call-done = bf16[1,1024,3584]{2,1,0:T(8,128)(2,1)} async-done(((bf16[1,128,3584]{2,1,0:T(8,128)(2,1)}), bf16[1,1024,3584]{2,1,0:T(8,128)(2,1)}) %all-gather.3.cloned.1.call-update) | async-done | bytes 7340048 | tf_op jit(solution)/shard_map/all_gather | solution.py:80
  88.6 101.4 %all-to-all-done.1 = bf16[64,8,3584]{2,1,0:T(8,128)(2,1)} async-done(((bf16[64,8,3584]{2,1,0:T(8,128)(2,1)}), bf16[64,8,3584]{2,1,0:T(8,128)(2,1)}, u32[]{:S(2)}, u32[]{:S(2)}) %all-to-all-start.1) | async-done | bytes 3670048 | tf_op jit(solution)/shard_map/all_to_all | solution.py:74
  190.0 8.4 fusion.3
  198.4 0.7 all_to_all.20
  199.2 13.7 %all-to-all-start.2 = ((f32[64,1,8]{2,1,0:T(1,128)}), f32[64,1,8]{2,1,0:T(1,128)S(1)}, u32[]{:S(2)}, u32[]{:S(2)}) async-start(f32[64,1,8]{2,1,0:T(1,128)} %bitcast.12), calls=%async_computation.2 | async-start | bytes 65536 | tf_op jit(solution)/shard_map/all_to_all | solution.py:88
  212.9 13.2 %all-to-all-done.2 = f32[64,1,8]{2,1,0:T(1,128)S(1)} async-done(((f32[64,1,8]{2,1,0:T(1,128)}), f32[64,1,8]{2,1,0:T(1,128)S(1)}, u32[]{:S(2)}, u32[]{:S(2)}) %all-to-all-start.2) | async-done | bytes 2080 | tf_op jit(solution)/shard_map/all_to_all | solution.py:88
  226.1 0.4 fusion.8
  226.7 4.0 convolution_bitcast_fusion
  230.7 4.7 copy.61
  235.4 0.4 fusion.11
  235.9 0.7 copy.52
  236.6 4.6 all-to-all-start
  241.2 13.2 %all-to-all-done = bf16[64,1,8]{2,1,0:T(2,128)(2,1)S(1)} async-done(((bf16[64,1,8]{2,1,0:T(2,128)(2,1)}), bf16[64,1,8]{2,1,0:T(2,128)(2,1)S(1)}, u32[]{:S(2)}, u32[]{:S(2)}) %all-to-all-start) | async-done | bytes 1056 | tf_op jit(solution)/shard_map/all_to_all | solution.py:75
  254.6 1.2 fusion.4
  255.8 660.8 %reduce-scatter.4.cloned.1.call-done = f32[56,192]{1,0:T(8,128)} async-done(((f32[3584,192]{1,0:T(8,128)}), f32[56,192]{1,0:T(8,128)}) %reduce-scatter.4.cloned.1.call-update) | async-done | bytes 43024 | tf_op jit(solution)/shard_map/reduce_scatter | solution.py:96
  916.6 0.8 convert_element_type.90
  917.4 24.6 %all-gather = bf16[448,192]{1,0:T(8,128)(2,1)S(1)} all-gather(bf16[56,192]{1,0:T(8,128)(2,1)S(1)} %convert_element_type.90), channel_id=2, replica_groups=mesh['dp'=8,'expert'=64] {'dp'}, dimensions={0}, use_global_device_ids=true | all-gather | bytes 193536 | tf_op jit(solution)/shard_map/all_gather | solution.py:12
  942.4 0.9 copy.62
  943.4 22.8 %psum.7 = bf16[56,192]{0,1:T(8,128)(2,1)S(1)} all-reduce(bf16[56,192]{0,1:T(8,128)(2,1)S(1)} %fusion.20), channel_id=1, replica_groups=mesh['dp'=8,'expert'=64] {'dp'}, use_global_device_ids=true, to_apply=%region_14.15 | all-reduce | flops 10752 | bytes 43008 | tf_op jit(solution)/shard_map/psum | solution.py:25
  966.1 0.6 dynamic-slice_convert_fusion
  (46 shorter events, 2.0 us)
Async XLA Ops:
  7.2 1.3 copy-start
  11.5 20.4 %copy-start.1 = (f32[128,192]{0,1:T(8,128)S(1)}, f32[128,192]{0,1:T(8,128)}, u32[]{:S(2)}) copy-start(f32[128,192]{0,1:T(8,128)} %param.10) | copy-start | bytes 294916
  11.5 20.4 %copy-start.3 = (s32[128,8]{0,1:T(8,128)S(1)}, s32[128,8]{0,1:T(8,128)}, u32[]{:S(2)}) copy-start(s32[128,8]{0,1:T(8,128)} %param.11) | copy-start | bytes 12292
  11.5 178.5 %all-to-all-start.1 = ((bf16[64,8,3584]{2,1,0:T(8,128)(2,1)}), bf16[64,8,3584]{2,1,0:T(8,128)(2,1)}, u32[]{:S(2)}, u32[]{:S(2)}) async-start(bf16[64,8,3584]{2,1,0:T(8,128)(2,1)} %convolution_convert_fusion), calls=%async_computation.1 | async-start | bytes 7340032 | tf_op jit(solution)/shard_map/all_to_all | solution.py:74
  31.2 57.5 %all-gather.3.cloned.1.call-start = ((), (), s32[]{:S(2)}) async-start(), calls=%async_computation.4 | async-start | bytes 8257536 | tf_op jit(solution)/shard_map/all_gather | solution.py:80
  199.2 26.9 %all-to-all-start.2 = ((f32[64,1,8]{2,1,0:T(1,128)}), f32[64,1,8]{2,1,0:T(1,128)S(1)}, u32[]{:S(2)}, u32[]{:S(2)}) async-start(f32[64,1,8]{2,1,0:T(1,128)} %bitcast.12), calls=%async_computation.2 | async-start | bytes 65536 | tf_op jit(solution)/shard_map/all_to_all | solution.py:88
  212.9 703.7 %reduce-scatter.4.cloned.1.call-start = ((), (), s32[]{:S(2)}) async-start(), calls=%async_computation.5 | async-start | bytes 3727360 | tf_op jit(solution)/shard_map/reduce_scatter | solution.py:96
  226.7 8.7 copy-start.2
  236.6 17.8 %all-to-all-start = ((bf16[64,1,8]{2,1,0:T(2,128)(2,1)}), bf16[64,1,8]{2,1,0:T(2,128)(2,1)S(1)}, u32[]{:S(2)}, u32[]{:S(2)}) async-start(bf16[64,1,8]{2,1,0:T(2,128)(2,1)} %copy.52), calls=%async_computation | async-start | bytes 65536 | tf_op jit(solution)/shard_map/all_to_all | solution.py:75
Sparse Core Ops, SparseCore 0:
  34.1 54.4 all-gather.2
  235.6 680.9 reduce-scatter.3
where the time goes:
time: 975 us; the launch traced here: 974 us
  waiting for transfers between devices  846 us (87%)
  blocking collectives  47.4 us (5%)
  starting transfers between devices  38 us (4%)
  matrix products  16.1 us (2%)
  between operations  14.2 us (1%)
    reduce_scatter x1, waiting for transfers between devices, local(): lax.psum_scatter(lax.dot_general(tokens_full, logit_grad, (((0,), (0,)),...  661 us
    all_to_all x1, waiting for transfers between devices, local(): lax.all_to_all(send_rows, 'expert', split_axis=0, concat_axis=0, tiled=True)  101 us
    all_gather x1, waiting for transfers between devices, local(): lax.all_gather(down_weight, 'dp', axis=1, tiled=True)[0]  56.4 us
    all_gather x1, blocking collectives, entering(): everything = lax.all_gather(shard.astype(jnp.bfloat16), axis)  24.6 us
    psum x1, blocking collectives, from_root(): return lax.psum(kept, axis)  22.8 us
    all_to_all x1, starting transfers between devices, local(): lax.all_to_all(send_rows, 'expert', split_axis=0, concat_axis=0, tiled=True)  19.6 us
  transfers between devices with their start and end apart: 5, of which 5 were waited for; matrix products, arithmetic and copies ran while one was open for 0% of the time, Pallas kernels for 0%

commit v1 on v0

v1 whole, which is shorter than its diff:
```python
import functools

import jax
import jax.numpy as jnp
from jax import lax
from jax.experimental import pallas as pl
from jax.experimental.pallas import tpu as pltpu
from jax.sharding import PartitionSpec as P

RSCALE = 2.827
ZLOSS = 0.25
NC = 2
MESH = pl.DeviceIdType.MESH
F32 = jnp.float32
BF16 = jnp.bfloat16


def drain(ref, sem):
    pltpu.make_async_copy(ref, ref, sem).wait()


def iota(shape, dim):
    return lax.broadcasted_iota(jnp.int32, shape, dim)


def kernel(
    dims,
    og, logits, ids, tok, w, saved,
    hid, lg, rg,
    send, recv, wfull, tokg, savedv, gsend, grecv, rsend, rrecv, lgs, lgb, lhs, zsend, zrecv, zterm, posv, small,
    row_r, row_s, gate_r, gate_s, ret_r, ret_s, wx_s, wx_r, wc_s, wc_r,
    t1_s, t1_r, tx_s, tx_r, tc_s, tc_r, lg_s, lg_r, z_s, z_r, local_sem,
):
    NX, NY, NZ = dims
    NDP, NE, NG = NX * NC, NY * NZ, NZ // 2
    GS = NY * 2
    D = og.shape[1]
    H = D // 2
    Q = D // NY
    FW = wfull.shape[0]
    FS = FW // NDP
    EX = logits.shape[1]
    ED = EX // NDP
    R = D // NE
    dp, e = lax.axis_index("dp"), lax.axis_index("expert")
    x, core = dp // NC, dp % NC
    y, z = e // NZ, e % NZ
    m0 = z // 2
    place = m0 * GS + y * 2 + z % 2

    def remote(src, dst, s, r, dev):
        return pltpu.make_async_remote_copy(
            src_ref=src, dst_ref=dst, send_sem=s, recv_sem=r, device_id=dev, device_id_type=MESH
        )

    barrier = pltpu.get_barrier_semaphore()

    def greet(i, c):
        pl.semaphore_signal(barrier, inc=1, device_id=(dp, lax.rem(e + i, NE)), device_id_type=MESH)
        return c

    lax.fori_loop(1, NE, greet, 0)

    def greet2(i, c):
        other = lax.rem(dp + 1 + i // NY, NDP)
        pl.semaphore_signal(barrier, inc=1, device_id=(other, lax.rem(i, NY) * NZ + z), device_id_type=MESH)
        return c

    lax.fori_loop(0, (NDP - 1) * NY, greet2, 0)
    load = pltpu.make_async_copy(saved, savedv, local_sem.at[0])
    load.start()
    own_w = pltpu.make_async_copy(w, wfull.at[pl.ds(pl.multiple_of(dp * FS, FS), FS)], local_sem.at[1])
    own_w.start()

    full = logits[...]
    if EX > 128:
        lt = jnp.concatenate([full[:, :128].T, full[:, EX - 128 :].T[256 - EX :]], axis=0)
    else:
        lt = full.T
    top = jnp.max(lt, axis=0, keepdims=True)
    shifted = jnp.exp(lt - top)
    total = jnp.sum(shifted, axis=0, keepdims=True)
    lse = top + jnp.log(total)
    zterm[...] = (2.0 * ZLOSS) * lse * (shifted / total)
    T = lt.shape[1]
    names = iota((EX, T), 0)
    k_rows = [ids[k : k + 1, :] for k in range(ids.shape[0])]
    chosen = jnp.concatenate(
        [jnp.sum(jnp.where(names == row, lt, 0.0), axis=0, keepdims=True) for row in k_rows], axis=0
    )
    scores = 1.0 / (1.0 + jnp.exp(-chosen))
    ssum = jnp.sum(scores, axis=0, keepdims=True)
    gates = RSCALE * scores / ssum
    small[0] = scores
    small[1] = gates
    small[2] = jnp.broadcast_to(ssum, scores.shape)
    gate_half = gates.astype(BF16).astype(F32)
    window = iota((NE, T), 0)
    mask = jnp.zeros((NE, T), F32)
    gate_e = jnp.zeros((NE, T), F32)
    for k, row in enumerate(k_rows):
        hit = window == row
        mask = jnp.where(hit, 1.0, mask)
        gate_e = jnp.where(hit, gate_half[k : k + 1, :], gate_e)
    earlier = (iota((T, T), 0) < iota((T, T), 1)).astype(F32).astype(BF16)
    rank = jnp.dot(mask.astype(BF16), earlier, preferred_element_type=F32)
    pos = jnp.where(mask > 0.0, rank, 255.0)
    posv[...] = pos
    lane = iota((NE, T), 1)
    slot_gates = jnp.zeros((NE, T), F32)
    for c in range(8):
        v = jnp.sum(jnp.where(pos == float(c), gate_e, 0.0), axis=1, keepdims=True)
        slot_gates = jnp.where(lane == c, v, slot_gates)
    gsend[...] = slot_gates[:, None, :]
    pos_half = pos.astype(BF16)

    pl.semaphore_wait(barrier, NE - 1 + (NDP - 1) * NY)

    own_w.wait()

    def w_rows(owner):
        return wfull.at[pl.ds(pl.multiple_of(owner * FS, FS), FS)]

    def tok_cols(yy):
        return tok.at[:, pl.ds(pl.multiple_of(yy * Q, 128), Q)]

    pair = (x * NC + 1 - core, e)
    for d in range(1, NX):
        remote(w_rows(dp), w_rows(dp), wx_s.at[d - 1], wx_r.at[d - 1], (lax.rem(x + d, NX) * NC + core, e)).start()
    remote(w_rows(dp), w_rows(dp), wc_s.at[0], wc_r.at[0], pair).start()
    for d in range(1, NY):
        yy = lax.rem(y + d, NY)
        remote(tok_cols(yy), tokg.at[dp, y], t1_s, t1_r, (dp, yy * NZ + z)).start()
    pltpu.make_async_copy(tok_cols(y), tokg.at[dp, y], t1_r).start()

    def order(i):
        half = (i + 1) // 2
        return lax.rem(m0 + NG // 2 + jnp.where(i % 2 == 1, NG - half, half), NG)

    def send_group(i, c):
        m = order(i)
        jj = iota((GS * 16, NE), 0) // 16
        ex = jj // 2 * NZ + 2 * m + jj % 2
        pick = (iota((GS * 16, NE), 1) == ex).astype(F32).astype(BF16)
        spread = jnp.dot(pick, pos_half, preferred_element_type=F32)
        row = iota((GS * 16, T), 0)
        table = (spread == (row % 8).astype(F32)).astype(F32).astype(BF16)
        first = iota((GS * 16, 1), 0) % 16 < 8
        a = jnp.dot(table, og[:, :H], preferred_element_type=F32)
        b = jnp.dot(table, og[:, H:], preferred_element_type=F32)
        send[m] = jnp.where(first, a, b).astype(BF16).reshape(GS, 16, H)

        def one(j, c2):
            to = j // 2 * NZ + 2 * m + j % 2

            @pl.when(to != e)
            def _():
                remote(send.at[m, j], recv.at[m0, y * 2 + z % 2], row_s, row_r.at[m0], (dp, to)).start()
                remote(gsend.at[to], grecv.at[place], gate_s, gate_r, (dp, to)).start()

            @pl.when(to == e)
            def _():
                pltpu.make_async_copy(send.at[m, j], recv.at[m, j], row_r.at[m]).start()
                pltpu.make_async_copy(gsend.at[e], grecv.at[place], gate_r).start()

            return c2

        return lax.fori_loop(0, GS, one, c)

    lax.fori_loop(0, NG, send_group, 0)

    for d in range(1, NX):
        shard = lax.rem(x + NX - d, NX) * NC + core
        remote(w_rows(shard), w_rows(shard), wx_s.at[d - 1], wx_r.at[d - 1], pair).wait_recv()
        remote(w_rows(shard), w_rows(shard), wc_s.at[d], wc_r.at[d], pair).start()
    drain(tokg.at[dp], t1_r)
    for d in range(1, NX):
        remote(tokg.at[dp], tokg.at[dp], tx_s.at[d - 1], tx_r.at[d - 1], (lax.rem(x + d, NX) * NC + core, e)).start()
    remote(tokg.at[dp], tokg.at[dp], tc_s.at[0], tc_r.at[0], pair).start()
    for d in range(NX):
        shard = lax.rem(x + NX - d, NX) * NC + 1 - core
        drain(w_rows(shard), wc_r.at[d])
    load.wait()
    drain(grecv, gate_r)

    lane8 = iota((GS, 8, 128), 2) == iota((GS, 8, 128), 1)
    FC = min(FW, 256)

    def work(i, c):
        m = order(i)
        drain(recv.at[m], row_r.at[m])
        rows = recv[m].reshape(GS * 16, H)
        gate_col = jnp.sum(
            jnp.where(lane8, grecv[pl.ds(pl.multiple_of(m * GS, GS), GS)], 0.0), axis=2, keepdims=True
        )
        span = pl.ds(pl.multiple_of(m * 16, 16), 16)
        back = jnp.zeros((GS, 8, 1), F32)
        nt = (((1,), (1,)), ((), ()))
        for f in range(0, FW, FC):
            a = lax.dot_general(rows, wfull[f : f + FC, :H], nt, preferred_element_type=F32)
            b = lax.dot_general(rows, wfull[f : f + FC, H:], nt, preferred_element_type=F32)
            g = a.reshape(GS, 16, FC)[:, :8] + b.reshape(GS, 16, FC)[:, 8:]
            hid[:, span, f : f + FC] = (gate_col * g).reshape(NY, 16, FC).astype(BF16)
            kept = savedv[:, span, f : f + FC].astype(F32).reshape(GS, 8, FC)
            back = back + jnp.sum(kept * g, axis=2, keepdims=True)
        rsend[pl.ds(pl.multiple_of(m * GS, GS), GS)] = jnp.sum(jnp.where(lane8, back, 0.0), axis=1, keepdims=True)

        def one(j, c2):
            to = j // 2 * NZ + 2 * m + j % 2

            @pl.when(to != e)
            def _():
                remote(rsend.at[m * GS + j], rrecv.at[e], ret_s, ret_r, (dp, to)).start()

            @pl.when(to == e)
            def _():
                pltpu.make_async_copy(rsend.at[m * GS + j], rrecv.at[e], ret_r).start()

            return c2

        return lax.fori_loop(0, GS, one, c)

    lax.fori_loop(0, NG // 2, work, 0)
    for d in range(1, NX):
        shard = lax.rem(x + NX - d, NX) * NC + core
        drain(tokg.at[shard], tx_r.at[d - 1])
        remote(tokg.at[shard], tokg.at[shard], tc_s.at[d], tc_r.at[d], pair).start()
    lax.fori_loop(NG // 2, NG, work, 0)
    for d in range(NX):
        shard = lax.rem(x + NX - d, NX) * NC + 1 - core
        drain(tokg.at[shard], tc_r.at[d])

    drain(rrecv, ret_r)
    ret = rrecv[...].reshape(NE, 128)
    pos = posv[...]
    grad_e = jnp.zeros((NE, T), F32)
    for c in range(8):
        grad_e = jnp.where(pos == float(c), ret[:, c : c + 1], grad_e)
    scores, gates, ssum = small[0], small[1], small[2]
    k_rows = [ids[k : k + 1, :] for k in range(ids.shape[0])]
    window = iota((NE, T), 0)
    choice = jnp.concatenate(
        [jnp.sum(jnp.where(window == row, grad_e, 0.0), axis=0, keepdims=True) for row in k_rows], axis=0
    )
    mixed = jnp.sum(choice * gates, axis=0, keepdims=True) / RSCALE
    dchosen = RSCALE / ssum * (choice - mixed) * scores * (1.0 - scores)
    names = iota((EX, T), 0)
    lgt = zterm[...]
    for k, row in enumerate(k_rows):
        lgt = lgt + jnp.where(names == row, dchosen[k : k + 1, :], 0.0)
    for d in range(NDP):
        lgs[d] = lgt[d * ED : (d + 1) * ED]

    mine = dp * NY + y

    def spread_lg(i, c):
        to_dp, to_y = lax.rem(dp + i // NY, NDP), lax.rem(y + i, NY)
        remote(lgs.at[to_dp], lgb.at[mine], lg_s, lg_r, (to_dp, to_y * NZ + z)).start()
        return c

    lax.fori_loop(1, NDP * NY, spread_lg, 0)
    pltpu.make_async_copy(lgs.at[dp], lgb.at[mine], lg_r).start()
    if EX > 128:
        lg[:, :128] = lgt[:128].T
        lg[:, 128:] = lgt[EX - 128 :].T[:, 256 - EX :]
    else:
        lg[...] = lgt.T
    drain(lgb, lg_r)
    for s in range(NDP * NY):
        v = lgb[s]
        hi = v.astype(BF16)
        lhs[:, s * T : (s + 1) * T] = jnp.concatenate([v, v - hi.astype(F32)], axis=0).astype(BF16)
    panel = jnp.zeros((2 * ED, Q), F32)
    for d in range(NDP):
        panel = panel + jnp.dot(
            lhs[:, d * NY * T : (d + 1) * NY * T], tokg[d].reshape(NY * T, Q), preferred_element_type=F32
        )
    panel = panel[:ED] + panel[ED:]
    for j in range(NZ):
        zsend[j, :, :R] = panel[:, j * R : (j + 1) * R]
        if R < 128:
            zsend[j, :, R:] = jnp.zeros((ED, 128 - R), F32)

    def spread_z(i, c):
        to = lax.rem(z + i, NZ)
        remote(zsend.at[to], zrecv.at[z], z_s, z_r, (dp, y * NZ + to)).start()
        return c

    lax.fori_loop(1, NZ, spread_z, 0)
    pltpu.make_async_copy(zsend.at[z], zrecv.at[z], z_r).start()
    drain(zrecv, z_r)
    out = zrecv[0]
    for j in range(1, NZ):
        out = out + zrecv[j]
    out = jnp.concatenate([out, jnp.zeros((128 - ED, 128), F32)], axis=0).T
    rg[...] = out[:R, :ED]

    drain(send.at[pl.ds(0, NG - 1)], row_s)
    drain(send.at[0, pl.ds(0, GS - 1)], row_s)
    drain(gsend.at[pl.ds(0, NE - 1)], gate_s)
    drain(rsend.at[pl.ds(0, NE - 1)], ret_s)
    for d in range(NX - 1):
        drain(w_rows(dp), wx_s.at[d])
        drain(tokg.at[dp], tx_s.at[d])
    for d in range(NX):
        drain(w_rows(dp), wc_s.at[d])
        drain(tokg.at[dp], tc_s.at[d])
    drain(tokg.at[dp, pl.ds(0, NY - 1)], t1_s)
    drain(lgb.at[pl.ds(0, NDP * NY - 1)], lg_s)
    drain(zsend.at[pl.ds(0, NZ - 1)], z_s)


def local(dims, tokens_in, out_grad, router_logits, expert_ids, saved_hidden, down_weight):
    NX, NY, NZ = dims
    NDP, NE, NG, GS = NX * NC, NY * NZ, NZ // 2, NY * 2
    T, D = out_grad.shape
    FW = saved_hidden.shape[4]
    EX = router_logits.shape[1]
    ED, Q, R = EX // NDP, D // NY, D // NE
    vmem = pl.BlockSpec(memory_space=pltpu.VMEM)
    hbm = pl.BlockSpec(memory_space=pl.ANY)
    dma = pltpu.SemaphoreType.DMA
    one = dma(())
    hid, lg, rg = pl.pallas_call(
        functools.partial(kernel, dims),
        out_shape=(
            jax.ShapeDtypeStruct((NY, NZ * 8, FW), BF16),
            jax.ShapeDtypeStruct((T, EX), F32),
            jax.ShapeDtypeStruct((R, ED), F32),
        ),
        in_specs=[vmem, vmem, vmem, hbm, hbm, hbm],
        out_specs=(vmem, vmem, vmem),
        scratch_shapes=[
            pltpu.VMEM((NG, GS, 16, D // 2), BF16),
            pltpu.VMEM((NG, GS, 16, D // 2), BF16),
            pltpu.VMEM((FW, D), BF16),
            pltpu.VMEM((NDP, NY, T, Q), BF16),
            pltpu.VMEM((NY, NZ * 8, FW), BF16),
            pltpu.VMEM((NE, 1, 128), F32),
            pltpu.VMEM((NE, 1, 128), F32),
            pltpu.VMEM((NE, 1, 128), F32),
            pltpu.VMEM((NE, 1, 128), F32),
            pltpu.VMEM((NDP, ED, T), F32),
            pltpu.VMEM((NDP * NY, ED, T), F32),
            pltpu.VMEM((2 * ED, NDP * NY * T), BF16),
            pltpu.VMEM((NZ, ED, 128), F32),
            pltpu.VMEM((NZ, ED, 128), F32),
            pltpu.VMEM((EX, T), F32),
            pltpu.VMEM((NE, T), F32),
            pltpu.VMEM((3, 8, T), F32),
            dma((NG,)), one, one, one, one, one,
            dma((NX - 1,)), dma((NX - 1,)), dma((NX,)), dma((NX,)),
            one, one, dma((NX - 1,)), dma((NX - 1,)), dma((NX,)), dma((NX,)),
            one, one, one, one, dma((2,)),
        ],
        compiler_params=pltpu.CompilerParams(
            collective_id=0, has_side_effects=True, vmem_limit_bytes=56 * 2**20
        ),
        cost_estimate=pl.CostEstimate(flops=4 * 10**9, bytes_accessed=6 * 10**6, transcendentals=0),
    )(
        out_grad,
        router_logits,
        expert_ids.T,
        tokens_in,
        down_weight.reshape(FW // NDP, D),
        saved_hidden.reshape(NY, NZ * 8, FW),
    )
    return hid.reshape(1, 1, NE, 8, FW), lg, rg


def solution(mesh, dims=(4, 4, 16)):
    in_specs = (
        P(("dp", "expert"), None),
        P(("dp", "expert"), None),
        P(("dp", "expert"), None),
        P(("dp", "expert"), None),
        P("dp", "expert", None, None, None),
        P("expert", "dp", None),
    )
    out_specs = (P("dp", "expert", None, None, None), P(("dp", "expert"), None), P("expert", "dp"))
    return jax.shard_map(
        functools.partial(local, dims), mesh=mesh, in_specs=in_specs, out_specs=out_specs, check_vma=False
    )
```

time: 975 us -> 242 us (0.25)
  waiting for transfers between devices: 846 us -> 0 us
  Pallas kernels: 0 us -> 234 us
  blocking collectives: 47.4 us -> 0 us
  starting transfers between devices: 38 us -> 0 us
  matrix products: 16.1 us -> 0 us
  between operations: 14.2 us -> 0.64 us
    reduce_scatter x1 -> x0, waiting for transfers between devices: 661 us -> none  [local(): lax.psum_scatter(lax.dot_general(tokens_full, logit_grad, (((0,), (0,)),...]
    pallas_call x0 -> x1, Pallas kernels: none -> 234 us  [local(): pl.pallas_call(functools.partial(kernel, dims), out_shape=(jax.ShapeDtype...]
    all_to_all x3 -> x0, waiting for transfers between devices: 128 us -> none  [the longest x1 101 us: local(): lax.all_to_all(send_rows, 'expert', split_axis=0, concat_axis=0, tiled=True)]
    all_gather x1 -> x0, waiting for transfers between devices: 56.4 us -> none  [local(): lax.all_gather(down_weight, 'dp', axis=1, tiled=True)[0]]
    all_to_all x3 -> x0, starting transfers between devices: 37.9 us -> none  [the longest x1 19.6 us: local(): lax.all_to_all(send_rows, 'expert', split_axis=0, concat_axis=0, tiled=True)]
    all_gather x1 -> x0, blocking collectives: 24.6 us -> none  [entering(): everything = lax.all_gather(shard.astype(jnp.bfloat16), axis)]
    psum x1 -> x0, blocking collectives: 22.8 us -> none  [from_root(): return lax.psum(kept, axis)]
    dot_general x5 -> x0, matrix products: 16.1 us -> none  [the longest x1 8.41 us: local(): lax.dot_general(flat_rows, lax.all_gather(down_weight, 'dp', axis=1, tile...]
  transfers between devices with their start and end apart: 5 -> 0, of which waited for: 5 -> 0; matrix products, arithmetic and copies ran while one was open for 0% -> 0% of each run, Pallas kernels for 0% -> 0%
where the time goes in v1:
time: 242 us; the launch traced here: 241 us
  Pallas kernels  234 us (97%)
  local copies, waits for them, and re-layouts  6.97 us (3%)
    pallas_call x1, Pallas kernels, local(): pl.pallas_call(functools.partial(kernel, dims), out_shape=(jax.ShapeDtype...  234 us
    unnamed x4, local copies, waits for them, and re-layouts  6.97 us

profile of v1, /device:TPU:1, one launch (start us, length us, event | category | flops | bytes accessed | tf_op | source)
XLA Modules:
  0.0 241.2 jit_solution(9951836716593300691)
XLA Ops:
  0.6 1.6 copy.9.logits
  2.3 233.6 %shard_map.85 = (bf16[4,128,1024]{2,1,0:T(8,128)(2,1)}, f32[128,192]{1,0:T(8,128)}, f32[56,24]{1,0:T(8,128)}) custom-call(bf16[128,3584]{1,0:T(8,128)(2,1)} %og.1, f32[128,192]{1,0:T(8,128)} %copy.9.logits, s32[8,128]{1,0:T(8,128)} %bitcast.7, bf16[128,3584]{1,0:T(8,128)(2,1)} %tok.1, bf16[128,3584]{1,0:T(8,128)(2,1)} %bitcast.6, bf16[4,128,1024]{2,1,0:T(8,128)(2,1)} %bitcast.5), custom_call_target="tpu_custom_call" | custom-call | flops 4000000000 | bytes 6000000 | tf_op jit(solution)/shard_map/pallas_call | solution.py:324
  235.9 1.4 copy.11
  237.3 1.6 copy.10
  239.0 2.3 copy.13

commit v2 on v1

v2 whole, which is shorter than its diff:
```python
import functools

import jax
import jax.numpy as jnp
from jax import lax
from jax.experimental import pallas as pl
from jax.experimental.pallas import tpu as pltpu
from jax.sharding import PartitionSpec as P

RSCALE = 2.827
ZLOSS = 0.25
NC = 2
MESH = pl.DeviceIdType.MESH
F32 = jnp.float32
BF16 = jnp.bfloat16


def drain(ref, sem):
    pltpu.make_async_copy(ref, ref, sem).wait()


def iota(shape, dim):
    return lax.broadcasted_iota(jnp.int32, shape, dim)


def kernel(
    dims,
    og, logits, ids, tok, w, saved,
    hid, lg, rg,
    ring, meta, nsend, nrecv, fsend, frecv, ftable, gnsend, gnrecv, gfsend, gfrecv, half,
    wfull, tokg, savedv, savedf, hidf, rsend, rrecv, lgb, lhs, zsend, zrecv, zterm, posv, small,
    ring_s, ring_r, meta_s, meta_r, near_s, near_r, gn_s, gn_r, far_s, far_r, gf_s, gf_r, ret_s, ret_r,
    wx_s, wx_r, wc_s, wc_r, t1_s, t1_r, tx_s, tx_r, tc_s, tc_r, lg_s, lg_r, z_s, z_r, local_sem,
):
    NX, NY, NZ = dims
    NDP, NE = NX * NC, NY * NZ
    RE = NZ // 4
    NN, NF = 2 * RE + 1, 2 * RE - 1
    T, D = og.shape
    H = D // 2
    Q = D // NY
    FW = wfull.shape[0]
    FS = FW // NDP
    FC = min(FW, 256)
    EX = logits.shape[0]
    ED = EX // NDP
    R = D // NE
    dp, e = lax.axis_index("dp"), lax.axis_index("expert")
    x, core = dp // NC, dp % NC
    y, z = e // NZ, e % NZ
    nt = (((1,), (1,)), ((), ()))

    def remote(src, dst, s, r, dev):
        return pltpu.make_async_remote_copy(
            src_ref=src, dst_ref=dst, send_sem=s, recv_sem=r, device_id=dev, device_id_type=MESH
        )

    barrier = pltpu.get_barrier_semaphore()

    def greet(i, c):
        pl.semaphore_signal(barrier, inc=1, device_id=(dp, lax.rem(e + i, NE)), device_id_type=MESH)
        return c

    lax.fori_loop(1, NE, greet, 0)

    def greet2(i, c):
        other = lax.rem(dp + 1 + i // NY, NDP)
        pl.semaphore_signal(barrier, inc=1, device_id=(other, lax.rem(i, NY) * NZ + z), device_id_type=MESH)
        return c

    lax.fori_loop(0, (NDP - 1) * NY, greet2, 0)
    load = pltpu.make_async_copy(saved, savedv, local_sem.at[0])
    load.start()
    own_w = pltpu.make_async_copy(w, wfull.at[pl.ds(pl.multiple_of(dp * FS, FS), FS)], local_sem.at[1])
    own_w.start()

    lt = logits[...]
    top = jnp.max(lt, axis=0, keepdims=True)
    shifted = jnp.exp(lt - top)
    total = jnp.sum(shifted, axis=0, keepdims=True)
    lse = top + jnp.log(total)
    zterm[...] = (2.0 * ZLOSS) * lse * (shifted / total)
    names = iota((EX, T), 0)
    k_rows = [ids[k : k + 1, :] for k in range(8)]
    chosen = jnp.concatenate(
        [jnp.sum(jnp.where(names == row, lt, 0.0), axis=0, keepdims=True) for row in k_rows], axis=0
    )
    scores = 1.0 / (1.0 + jnp.exp(-chosen))
    ssum = jnp.sum(scores, axis=0, keepdims=True)
    gates = RSCALE * scores / ssum
    small[0] = scores
    small[1] = gates
    small[2] = jnp.broadcast_to(ssum, scores.shape)
    own_meta = meta.at[2 * RE]
    own_meta[0:8] = ids[...].astype(F32)
    own_meta[8:16] = gates.astype(BF16).astype(F32)
    lane8 = iota((NY, 8, 128), 2) == iota((NY, 8, 128), 1)

    def slots(info):
        window = iota((NE, T), 0).astype(F32)
        mask = jnp.zeros((NE, T), F32)
        gate = jnp.zeros((NE, T), F32)
        for k in range(8):
            hit = window == info[k : k + 1, :]
            mask = jnp.where(hit, 1.0, mask)
            gate = jnp.where(hit, info[8 + k : 9 + k, :], gate)
        earlier = (iota((T, T), 0) < iota((T, T), 1)).astype(F32).astype(BF16)
        rank = jnp.dot(mask.astype(BF16), earlier, preferred_element_type=F32)
        return jnp.where(mask > 0.0, rank, 255.0), gate

    def tables(pos, gate, experts):
        n = experts.shape[0]
        pick = (iota((n, NE), 1) == experts).astype(F32).astype(BF16)
        spread = jnp.dot(pick, pos.astype(BF16), preferred_element_type=F32)
        hit = spread == (iota((n, T), 0) % 8).astype(F32)
        gates_at = jnp.dot(pick, gate.astype(BF16), preferred_element_type=F32)
        col = jnp.sum(jnp.where(hit, gates_at, 0.0), axis=1, keepdims=True).reshape(n // 8, 8, 1)
        at = iota((n // 8, 8, 128), 2) == iota((n // 8, 8, 128), 1)
        return hit.astype(F32).astype(BF16), jnp.sum(jnp.where(at, col, 0.0), axis=1, keepdims=True)

    def dispatch(ni, low, high, pos, gate):
        experts = iota((NY * 8, 1), 0) // 8 * NZ + z
        table, rows = tables(pos, gate, experts)
        gnsend[ni] = rows
        a = jnp.dot(table, low, preferred_element_type=F32).reshape(NY, 8, H)
        b = jnp.dot(table, high, preferred_element_type=F32).reshape(NY, 8, H)
        nsend[ni] = jnp.concatenate([a, b], axis=1).astype(BF16)
        for d in range(1, NY):
            yy = lax.rem(y + d, NY)
            remote(nsend.at[ni, yy], nrecv.at[ni, y], near_s, near_r.at[ni], (dp, yy * NZ + z)).start()
            remote(gnsend.at[ni, yy], gnrecv.at[ni, y], gn_s, gn_r.at[ni], (dp, yy * NZ + z)).start()
        pltpu.make_async_copy(nsend.at[ni, y], nrecv.at[ni, y], near_r.at[ni]).start()
        pltpu.make_async_copy(gnsend.at[ni, y], gnrecv.at[ni, y], gn_r.at[ni]).start()

    def hop(g, st, c):
        to = (dp, y * NZ + lax.rem(z + (1 if g == 0 else NZ - 1), NZ))
        src = og.at[:, pl.ds(c * H, H)] if st == 0 else ring.at[g, st - 1, c]
        remote(src, ring.at[g, st, c], ring_s.at[g, st, c], ring_r.at[g, st, c], to).start()
        if c == 0:
            info = own_meta if st == 0 else meta.at[g * RE + st - 1]
            remote(info, meta.at[g * RE + st], meta_s.at[g, st], meta_r.at[g, st], to).start()

    def arrived(g, st, c):
        if c == 0:
            drain(meta.at[g * RE + st], meta_r.at[g, st])
        drain(ring.at[g, st, c], ring_r.at[g, st, c])

    def relay(g, c):
        n = RE * NY
        if c == 0:
            d = iota((n * 8, 1), 0) // 8
            step = d // NY + 1
            experts = (y + d % NY) % NY * NZ + (z + (step if g == 0 else NZ - step)) % NZ
            pos, gate = slots(meta[g * RE + RE - 1])
            table, rows = tables(pos, gate, experts)
            ftable[g] = table
            gfsend[g] = rows
        p = jnp.dot(ftable[g], ring[g, RE - 1, c], preferred_element_type=F32).reshape(n, 8, H)
        fsend[c, g] = jnp.concatenate([p[:, :, : H // 2], p[:, :, H // 2 :]], axis=1).astype(BF16)

        def one(d, carry):
            j = d // NY + 1
            to = (dp, lax.rem(y + d % NY, NY) * NZ + lax.rem(z + (j if g == 0 else NZ - j), NZ))
            fi = j - 1 if g == 0 else jnp.where(j == RE, RE - 1, RE - 1 + j)
            remote(fsend.at[c, g, d], frecv.at[c, fi, y], far_s, far_r.at[c], to).start()
            if c == 0:
                remote(gfsend.at[g, d], gfrecv.at[fi, y], gf_s, gf_r, to).start()
            return carry

        last = (RE - 1) * NY
        split = last + NY // 2
        lax.fori_loop(*((last, split) if g == 0 else (split, RE * NY)), one, 0)
        lax.fori_loop(0, last, one, 0)

    def w_rows(owner):
        return wfull.at[pl.ds(pl.multiple_of(owner * FS, FS), FS)]

    def tok_cols(yy):
        return tok.at[:, pl.ds(pl.multiple_of(yy * Q, 128), Q)]

    pair = (x * NC + 1 - core, e)
    own_w.wait()
    pl.semaphore_wait(barrier, NE - 1 + (NDP - 1) * NY)

    for c in range(2):
        for g in range(2):
            hop(g, 0, c)
    for d in range(1, NX):
        remote(w_rows(dp), w_rows(dp), wx_s.at[d - 1], wx_r.at[d - 1], (lax.rem(x + d, NX) * NC + core, e)).start()
    remote(w_rows(dp), w_rows(dp), wc_s.at[0], wc_r.at[0], pair).start()
    for d in range(1, NY):
        yy = lax.rem(y + d, NY)
        remote(tok_cols(yy), tokg.at[dp, y], t1_s, t1_r, (dp, yy * NZ + z)).start()
    pltpu.make_async_copy(tok_cols(y), tokg.at[dp, y], t1_r).start()

    pos, gate = slots(own_meta[...])
    posv[...] = pos
    dispatch(0, og[:, :H], og[:, H:], pos, gate)
    load.wait()
    savedf[...] = savedv[...].astype(F32).reshape(NY, NZ, 8, FW)

    for st in range(1, RE):
        for c in range(2):
            for g in range(2):
                arrived(g, st - 1, c)
                hop(g, st, c)
        for g in range(2):
            pos, gate = slots(meta[g * RE + st - 1])
            dispatch(2 * st - 1 + g, ring[g, st - 1, 0], ring[g, st - 1, 1], pos, gate)
        if st == max(RE - 2, 1):
            for d in range(1, NX):
                shard = lax.rem(x + NX - d, NX) * NC + core
                drain(w_rows(shard), wx_r.at[d - 1])
                remote(w_rows(shard), w_rows(shard), wc_s.at[d], wc_r.at[d], pair).start()
            drain(tokg.at[dp], t1_r)
            for d in range(1, NX):
                to = (lax.rem(x + d, NX) * NC + core, e)
                remote(tokg.at[dp], tokg.at[dp], tx_s.at[d - 1], tx_r.at[d - 1], to).start()
            remote(tokg.at[dp], tokg.at[dp], tc_s.at[0], tc_r.at[0], pair).start()

    def joined(block, n, width):
        v = block.astype(F32)
        low = v[:, :8].reshape(n * 8, width)
        high = v[:, 8:].reshape(n * 8, width)
        return jnp.concatenate([low, high], axis=1).astype(BF16)

    def finish(f, g, backs, columns, sources):
        for i, zs in enumerate(sources):
            part = g[i * NY * 8 : (i + 1) * NY * 8].reshape(NY, 8, FC)
            hidf[:, zs, :, f : f + FC] = columns[i] * part
            backs[i] = backs[i] + jnp.sum(savedf[:, zs, :, f : f + FC] * part, axis=2, keepdims=True)

    def column(rows):
        return jnp.sum(jnp.where(lane8, rows, 0.0), axis=2, keepdims=True)

    def give_back(i, zs, back):
        rsend[i] = jnp.sum(jnp.where(lane8, back, 0.0), axis=1, keepdims=True)
        for d in range(NY):
            yy = lax.rem(y + d, NY)
            if i == 0 and d == 0:
                pltpu.make_async_copy(rsend.at[i, yy], rrecv.at[e], ret_r).start()
            else:
                remote(rsend.at[i, yy], rrecv.at[e], ret_s, ret_r, (dp, yy * NZ + zs)).start()

    def near(group):
        sources = []
        for ni in group:
            drain(nrecv.at[ni], near_r.at[ni])
            drain(gnrecv.at[ni], gn_r.at[ni])
            st = (ni + 1) // 2
            sources.append(lax.rem(z + (NZ - st if ni % 2 == 1 else st), NZ))
        rows = jnp.concatenate([joined(nrecv[ni], NY, H) for ni in group], axis=0)
        columns = [column(gnrecv[ni]) for ni in group]
        backs = [jnp.zeros((NY, 8, 1), F32) for ni in group]
        for f in range(0, FW, FC):
            g = lax.dot_general(rows, wfull[f : f + FC], nt, preferred_element_type=F32)
            finish(f, g, backs, columns, sources)
        for ni, zs, back in zip(group, sources, backs):
            give_back(ni, zs, back)

    for c in range(2):
        for g in range(2):
            arrived(g, RE - 1, c)
            relay(g, c)
    for g in range(2):
        pos, gate = slots(meta[g * RE + RE - 1])
        dispatch(2 * RE - 1 + g, ring[g, RE - 1, 0], ring[g, RE - 1, 1], pos, gate)
    for d in range(NX):
        shard = lax.rem(x + NX - d, NX) * NC + 1 - core
        drain(w_rows(shard), wc_r.at[d])
    near([0, 1, 2])
    for first in range(3, NN, 4):
        near(list(range(first, min(first + 4, NN))))
    for d in range(1, NX):
        shard = lax.rem(x + NX - d, NX) * NC + core
        drain(tokg.at[shard], tx_r.at[d - 1])
        remote(tokg.at[shard], tokg.at[shard], tc_s.at[d], tc_r.at[d], pair).start()

    drain(frecv.at[0], far_r.at[0])
    rows = joined(frecv[0].reshape(NF * NY, 16, H // 2), NF * NY, H // 2)
    for f in range(0, FW, FC):
        half[:, f : f + FC] = lax.dot_general(rows, wfull[f : f + FC, :H], nt, preferred_element_type=F32)
    drain(gfrecv, gf_r)
    columns = [column(gfrecv[i]) for i in range(NF)]
    backs = [jnp.zeros((NY, 8, 1), F32) for i in range(NF)]
    sources = [lax.rem(z + (NZ - RE - 1 - i if i < RE else i + 1), NZ) for i in range(NF)]
    drain(frecv.at[1], far_r.at[1])
    rows = joined(frecv[1].reshape(NF * NY, 16, H // 2), NF * NY, H // 2)
    for f in range(0, FW, FC):
        g = lax.dot_general(rows, wfull[f : f + FC, H:], nt, preferred_element_type=F32)
        finish(f, g + half[:, f : f + FC], backs, columns, sources)
    for i in range(NF):
        give_back(NN + i, sources[i], backs[i])
    hid[...] = hidf[...].reshape(NY, NZ * 8, FW).astype(BF16)
    for d in range(NX):
        shard = lax.rem(x + NX - d, NX) * NC + 1 - core
        drain(tokg.at[shard], tc_r.at[d])

    drain(rrecv, ret_r)
    ret = rrecv[...].reshape(NE, 128)
    pos = posv[...]
    grad_e = jnp.zeros((NE, T), F32)
    for c in range(8):
        grad_e = jnp.where(pos == float(c), ret[:, c : c + 1], grad_e)
    scores, gates, ssum = small[0], small[1], small[2]
    k_rows = [ids[k : k + 1, :] for k in range(8)]
    window = iota((NE, T), 0)
    choice = jnp.concatenate(
        [jnp.sum(jnp.where(window == row, grad_e, 0.0), axis=0, keepdims=True) for row in k_rows], axis=0
    )
    mixed = jnp.sum(choice * gates, axis=0, keepdims=True) / RSCALE
    dchosen = RSCALE / ssum * (choice - mixed) * scores * (1.0 - scores)
    names = iota((EX, T), 0)
    lgt = zterm[...]
    for k, row in enumerate(k_rows):
        lgt = lgt + jnp.where(names == row, dchosen[k : k + 1, :], 0.0)
    lg[...] = lgt.reshape(NDP, ED, T)

    mine = dp * NY + y

    def spread_lg(i, c):
        to_dp, to_y = lax.rem(dp + i // NY, NDP), lax.rem(y + i, NY)
        remote(lg.at[to_dp], lgb.at[mine], lg_s, lg_r, (to_dp, to_y * NZ + z)).start()
        return c

    lax.fori_loop(1, NDP * NY, spread_lg, 0)
    pltpu.make_async_copy(lg.at[dp], lgb.at[mine], lg_r).start()
    drain(lgb, lg_r)
    for s in range(NDP * NY):
        v = lgb[s]
        hi = v.astype(BF16)
        lhs[:, s * T : (s + 1) * T] = jnp.concatenate([v, v - hi.astype(F32)], axis=0).astype(BF16)
    panel = jnp.zeros((2 * ED, Q), F32)
    for d in range(NDP):
        panel = panel + jnp.dot(
            lhs[:, d * NY * T : (d + 1) * NY * T], tokg[d].reshape(NY * T, Q), preferred_element_type=F32
        )
    panel = panel[:ED] + panel[ED:]
    for j in range(NZ):
        zsend[j, :, :R] = panel[:, j * R : (j + 1) * R]
        if R < 128:
            zsend[j, :, R:] = jnp.zeros((ED, 128 - R), F32)

    def spread_z(i, c):
        to = lax.rem(z + i, NZ)
        remote(zsend.at[to], zrecv.at[z], z_s, z_r, (dp, y * NZ + to)).start()
        return c

    lax.fori_loop(1, NZ, spread_z, 0)
    pltpu.make_async_copy(zsend.at[z], zrecv.at[z], z_r).start()
    drain(zrecv, z_r)
    out = zrecv[0]
    for j in range(1, NZ):
        out = out + zrecv[j]
    rg[...] = out[:, :R]

    for g in range(2):
        for st in range(RE):
            drain(meta.at[0], meta_s.at[g, st])
            for c in range(2):
                drain(ring.at[0, 0, 0], ring_s.at[g, st, c])
    drain(nsend.at[:, pl.ds(0, NY - 1)], near_s)
    drain(gnsend.at[:, pl.ds(0, NY - 1)], gn_s)
    drain(frecv, far_s)
    drain(gfrecv, gf_s)
    drain(rsend.at[pl.ds(1, NZ - 1)], ret_s)
    drain(rsend.at[0, pl.ds(0, NY - 1)], ret_s)
    for d in range(NX - 1):
        drain(w_rows(dp), wx_s.at[d])
        drain(tokg.at[dp], tx_s.at[d])
    for d in range(NX):
        drain(w_rows(dp), wc_s.at[d])
        drain(tokg.at[dp], tc_s.at[d])
    drain(tokg.at[dp, pl.ds(0, NY - 1)], t1_s)
    drain(lgb.at[pl.ds(0, NDP * NY - 1)], lg_s)
    drain(zsend.at[pl.ds(0, NZ - 1)], z_s)


def local(dims, tokens_in, out_grad, router_logits, expert_ids, saved_hidden, down_weight):
    NX, NY, NZ = dims
    NDP, NE = NX * NC, NY * NZ
    RE = NZ // 4
    NN, NF = 2 * RE + 1, 2 * RE - 1
    T, D = out_grad.shape
    H = D // 2
    FW = saved_hidden.shape[4]
    EX = router_logits.shape[1]
    ED, Q, R = EX // NDP, D // NY, D // NE
    vmem = pl.BlockSpec(memory_space=pltpu.VMEM)
    hbm = pl.BlockSpec(memory_space=pl.ANY)
    dma = pltpu.SemaphoreType.DMA
    one = dma(())
    hid, lg, rg = pl.pallas_call(
        functools.partial(kernel, dims),
        out_shape=(
            jax.ShapeDtypeStruct((NY, NZ * 8, FW), BF16),
            jax.ShapeDtypeStruct((NDP, ED, T), F32),
            jax.ShapeDtypeStruct((ED, R), F32),
        ),
        in_specs=[vmem, vmem, vmem, hbm, hbm, hbm],
        out_specs=(vmem, vmem, vmem),
        scratch_shapes=[
            pltpu.VMEM((2, RE, 2, T, H), BF16),
            pltpu.VMEM((2 * RE + 1, 16, T), F32),
            pltpu.VMEM((NN, NY, 16, H), BF16),
            pltpu.VMEM((NN, NY, 16, H), BF16),
            pltpu.VMEM((2, 2, RE * NY, 16, H // 2), BF16),
            pltpu.VMEM((2, NF, NY, 16, H // 2), BF16),
            pltpu.VMEM((2, RE * NY * 8, T), BF16),
            pltpu.VMEM((NN, NY, 1, 128), F32),
            pltpu.VMEM((NN, NY, 1, 128), F32),
            pltpu.VMEM((2, RE * NY, 1, 128), F32),
            pltpu.VMEM((NF, NY, 1, 128), F32),
            pltpu.VMEM((NF * NY * 8, FW), F32),
            pltpu.VMEM((FW, D), BF16),
            pltpu.VMEM((NDP, NY, T, Q), BF16),
            pltpu.VMEM((NY, NZ * 8, FW), BF16),
            pltpu.VMEM((NY, NZ, 8, FW), F32),
            pltpu.VMEM((NY, NZ, 8, FW), F32),
            pltpu.VMEM((NZ, NY, 1, 128), F32),
            pltpu.VMEM((NE, 1, 128), F32),
            pltpu.VMEM((NDP * NY, ED, T), F32),
            pltpu.VMEM((2 * ED, NDP * NY * T), BF16),
            pltpu.VMEM((NZ, ED, 128), F32),
            pltpu.VMEM((NZ, ED, 128), F32),
            pltpu.VMEM((EX, T), F32),
            pltpu.VMEM((NE, T), F32),
            pltpu.VMEM((3, 8, T), F32),
            dma((2, RE, 2)), dma((2, RE, 2)), dma((2, RE)), dma((2, RE)),
            one, dma((NN,)), one, dma((NN,)), one, dma((2,)), one, one, one, one,
            dma((NX - 1,)), dma((NX - 1,)), dma((NX,)), dma((NX,)),
            one, one, dma((NX - 1,)), dma((NX - 1,)), dma((NX,)), dma((NX,)),
            one, one, one, one, dma((2,)),
        ],
        compiler_params=pltpu.CompilerParams(
            collective_id=0, has_side_effects=True, vmem_limit_bytes=58 * 2**20
        ),
        cost_estimate=pl.CostEstimate(flops=4 * 10**9, bytes_accessed=6 * 10**6, transcendentals=0),
    )(
        out_grad,
        router_logits.T,
        expert_ids.T,
        tokens_in,
        down_weight.reshape(FW // NDP, D),
        saved_hidden.reshape(NY, NZ * 8, FW),
    )
    return hid.reshape(1, 1, NE, 8, FW), lg.reshape(EX, T).T, rg.T


def solution(mesh, dims=(4, 4, 16)):
    in_specs = (
        P(("dp", "expert"), None),
        P(("dp", "expert"), None),
        P(("dp", "expert"), None),
        P(("dp", "expert"), None),
        P("dp", "expert", None, None, None),
        P("expert", "dp", None),
    )
    out_specs = (P("dp", "expert", None, None, None), P(("dp", "expert"), None), P("expert", "dp"))
    return jax.shard_map(
        functools.partial(local, dims), mesh=mesh, in_specs=in_specs, out_specs=out_specs, check_vma=False
    )
```

time: 242 us -> 179 us (0.74)
  Pallas kernels: 234 us -> 174 us
  local copies, waits for them, and re-layouts: 6.97 us -> 3.61 us
    pallas_call x1, Pallas kernels: 234 us -> 174 us  [local(): pl.pallas_call(functools.partial(kernel, dims), out_shape=(jax.ShapeDtype...]
    unnamed x4 -> x7, local copies, waits for them, and re-layouts: 6.97 us -> 3.61 us
where the time goes in v2:
time: 179 us; the launch traced here: 178 us
  Pallas kernels  174 us (97%)
  local copies, waits for them, and re-layouts  3.61 us (2%)
    pallas_call x1, Pallas kernels, local(): pl.pallas_call(functools.partial(kernel, dims), out_shape=(jax.ShapeDtype...  174 us
    unnamed x7, local copies, waits for them, and re-layouts  3.61 us

profile of v2, /device:TPU:1, one launch (start us, length us, event | category | flops | bytes accessed | tf_op | source)
XLA Modules:
  0.0 178.3 jit_solution(8317684242402078858)
XLA Ops:
  0.6 174.1 %shard_map.85 = (bf16[4,128,1024]{2,1,0:T(8,128)(2,1)}, f32[8,24,128]{2,1,0:T(8,128)}, f32[24,56]{1,0:T(8,128)}) custom-call(bf16[128,3584]{1,0:T(8,128)(2,1)} %og.1, f32[192,128]{1,0:T(8,128)} %bitcast.14, s32[8,128]{1,0:T(8,128)} %bitcast.15, bf16[128,3584]{1,0:T(8,128)(2,1)} %tok.1, bf16[128,3584]{1,0:T(8,128)(2,1)} %bitcast.13, ...), custom_call_target="tpu_custom_call" | custom-call | flops 4000000000 | bytes 6000000 | tf_op jit(solution)/shard_map/pallas_call | solution.py:393
  174.7 0.0 copy-start
  174.7 2.3 %copy.12 = bf16[1,1,64,8,1024]{4,3,2,1,0:T(8,128)(2,1)} copy(bf16[1,1,64,8,1024]{4,3,2,1,0:T(8,128)(2,1)} %bitcast.9) | data formatting | bytes 2097152
  177.0 0.0 copy-done
  177.0 0.0 copy-start.1
  177.0 0.6 copy.13
  177.7 0.1 copy-done.1
  177.7 0.6 copy.14
Async XLA Ops:
  174.7 2.3 %copy-start = (f32[8,24,128]{2,1,0:T(8,128)S(1)}, f32[8,24,128]{2,1,0:T(8,128)}, u32[]{:S(2)}) copy-start(f32[8,24,128]{2,1,0:T(8,128)} %get-tuple-element.7) | copy-start | bytes 294916
  177.0 0.7 copy-start.1

commit v3 on v2

--- a/solution.py
+++ b/solution.py
@@ -25,24 +25,24 @@
 
 def kernel(
     dims,
-    og, logits, ids, tok, w, saved,
+    og_in, logits_in, ids_in, tok, w, saved,
     hid, lg, rg,
     ring, meta, nsend, nrecv, fsend, frecv, ftable, gnsend, gnrecv, gfsend, gfrecv, half,
-    wfull, tokg, savedv, savedf, hidf, rsend, rrecv, lgb, lhs, zsend, zrecv, zterm, posv, small,
+    wfull, tokg, savedv, savedf, hidf, rsend, rrecv, esend, erecv, dsend, drecv, zsend, zrecv, zterm, posv, small, og, logits, ids,
     ring_s, ring_r, meta_s, meta_r, near_s, near_r, gn_s, gn_r, far_s, far_r, gf_s, gf_r, ret_s, ret_r,
-    wx_s, wx_r, wc_s, wc_r, t1_s, t1_r, tx_s, tx_r, tc_s, tc_r, lg_s, lg_r, z_s, z_r, local_sem,
+    wx_s, wx_r, wc_s, wc_r, t1_s, t1_r, tx_s, tx_r, tc_s, tc_r, e_s, e_r, d_s, d_r, z_s, z_r, local_sem,
 ):
     NX, NY, NZ = dims
     NDP, NE = NX * NC, NY * NZ
     RE = NZ // 4
     NN, NF = 2 * RE + 1, 2 * RE - 1
-    T, D = og.shape
+    T, D = og_in.shape
     H = D // 2
     Q = D // NY
     FW = wfull.shape[0]
     FS = FW // NDP
     FC = min(FW, 256)
-    EX = logits.shape[0]
+    EX = logits_in.shape[0]
     ED = EX // NDP
     R = D // NE
     dp, e = lax.axis_index("dp"), lax.axis_index("expert")
@@ -55,6 +55,13 @@
             src_ref=src, dst_ref=dst, send_sem=s, recv_sem=r, device_id=dev, device_id_type=MESH
         )
 
+    loads = [
+        pltpu.make_async_copy(src, dst, local_sem.at[2 + i])
+        for i, (src, dst) in enumerate(((logits_in, logits), (ids_in, ids), (og_in, og)))
+    ]
+    for copy in loads:
+        copy.start()
+
     barrier = pltpu.get_barrier_semaphore()
 
     def greet(i, c):
@@ -74,6 +81,8 @@
     own_w = pltpu.make_async_copy(w, wfull.at[pl.ds(pl.multiple_of(dp * FS, FS), FS)], local_sem.at[1])
     own_w.start()
 
+    loads[0].wait()
+    loads[1].wait()
     lt = logits[...]
     top = jnp.max(lt, axis=0, keepdims=True)
     shifted = jnp.exp(lt - top)
@@ -92,11 +101,16 @@
     small[1] = gates
     small[2] = jnp.broadcast_to(ssum, scores.shape)
     own_meta = meta.at[2 * RE]
-    own_meta[0:8] = ids[...].astype(F32)
-    own_meta[8:16] = gates.astype(BF16).astype(F32)
+    names_f = ids[...].astype(F32)
+    own_meta[...] = jnp.concatenate([names_f, gates], axis=0).astype(BF16)
+    for d in range(NDP):
+        esend[d, :ED] = zterm[d * ED : (d + 1) * ED]
+        esend[d, ED:] = names_f
+    loads[2].wait()
     lane8 = iota((NY, 8, 128), 2) == iota((NY, 8, 128), 1)
 
     def slots(info):
+        info = info.astype(F32)
         window = iota((NE, T), 0).astype(F32)
         mask = jnp.zeros((NE, T), F32)
         gate = jnp.zeros((NE, T), F32)
@@ -170,7 +184,7 @@
         last = (RE - 1) * NY
         split = last + NY // 2
         lax.fori_loop(*((last, split) if g == 0 else (split, RE * NY)), one, 0)
-        lax.fori_loop(0, last, one, 0)
+        lax.fori_loop(0, last, lambda i, carry: one(last - 1 - i, carry), 0)
 
     def w_rows(owner):
         return wfull.at[pl.ds(pl.multiple_of(owner * FS, FS), FS)]
@@ -192,6 +206,16 @@
         yy = lax.rem(y + d, NY)
         remote(tok_cols(yy), tokg.at[dp, y], t1_s, t1_r, (dp, yy * NZ + z)).start()
     pltpu.make_async_copy(tok_cols(y), tokg.at[dp, y], t1_r).start()
+
+    mine = dp * NY + y
+
+    def spread_early(i, c):
+        to_dp, to_y = lax.rem(dp + i // NY, NDP), lax.rem(y + i, NY)
+        remote(esend.at[to_dp], erecv.at[mine], e_s, e_r, (to_dp, to_y * NZ + z)).start()
+        return c
+
+    lax.fori_loop(1, NDP * NY, spread_early, 0)
+    pltpu.make_async_copy(esend.at[dp], erecv.at[mine], e_r).start()
 
     pos, gate = slots(own_meta[...])
     posv[...] = pos
@@ -310,36 +334,47 @@
     )
     mixed = jnp.sum(choice * gates, axis=0, keepdims=True) / RSCALE
     dchosen = RSCALE / ssum * (choice - mixed) * scores * (1.0 - scores)
+    dsend[...] = dchosen
+
+    def spread_d(i, c):
+        to_dp, to_y = lax.rem(dp + i // NY, NDP), lax.rem(y + i, NY)
+        remote(dsend, drecv.at[mine], d_s, d_r.at[dp], (to_dp, to_y * NZ + z)).start()
+        return c
+
+    lax.fori_loop(1, NDP * NY, spread_d, 0)
+    pltpu.make_async_copy(dsend, drecv.at[mine], d_r.at[dp]).start()
     names = iota((EX, T), 0)
     lgt = zterm[...]
     for k, row in enumerate(k_rows):
         lgt = lgt + jnp.where(names == row, dchosen[k : k + 1, :], 0.0)
     lg[...] = lgt.reshape(NDP, ED, T)
 
-    mine = dp * NY + y
-
-    def spread_lg(i, c):
-        to_dp, to_y = lax.rem(dp + i // NY, NDP), lax.rem(y + i, NY)
-        remote(lg.at[to_dp], lgb.at[mine], lg_s, lg_r, (to_dp, to_y * NZ + z)).start()
-        return c
-
-    lax.fori_loop(1, NDP * NY, spread_lg, 0)
-    pltpu.make_async_copy(lg.at[dp], lgb.at[mine], lg_r).start()
-    drain(lgb, lg_r)
-    for s in range(NDP * NY):
-        v = lgb[s]
-        hi = v.astype(BF16)
-        lhs[:, s * T : (s + 1) * T] = jnp.concatenate([v, v - hi.astype(F32)], axis=0).astype(BF16)
+    drain(erecv, e_r)
+    own_names = (iota((ED, T), 0) + dp * ED).astype(F32)
     panel = jnp.zeros((2 * ED, Q), F32)
-    for d in range(NDP):
-        panel = panel + jnp.dot(
-            lhs[:, d * NY * T : (d + 1) * NY * T], tokg[d].reshape(NY * T, Q), preferred_element_type=F32
-        )
+    for i in range(NDP):
+        owner = lax.rem(dp + i, NDP)
+        drain(drecv.at[pl.ds(owner * NY, NY)], d_r.at[owner])
+        parts = []
+        for yy in range(NY):
+            at = owner * NY + yy
+            early, late = erecv[at], drecv[at]
+            v = early[:ED]
+            for k in range(8):
+                v = v + jnp.where(early[ED + k : ED + k + 1] == own_names, late[k : k + 1], 0.0)
+            parts.append(v)
+        v = jnp.concatenate(parts, axis=1)
+        hi = v.astype(BF16).astype(F32)
+        both = jnp.concatenate([v, v - hi], axis=0).astype(BF16)
+        panel = panel + jnp.dot(both, tokg[owner].reshape(NY * T, Q), preferred_element_type=F32)
     panel = panel[:ED] + panel[ED:]
+    blank = jnp.zeros((16, 64 - R), F32) if R < 64 else None
     for j in range(NZ):
-        zsend[j, :, :R] = panel[:, j * R : (j + 1) * R]
-        if R < 128:
-            zsend[j, :, R:] = jnp.zeros((ED, 128 - R), F32)
+        piece = panel[:, j * R : (j + 1) * R]
+        sides = [piece[:16], jnp.concatenate([piece[16:], jnp.zeros((32 - ED, R), F32)], axis=0)]
+        if R < 64:
+            sides = [sides[0], blank, sides[1], blank]
+        zsend[j] = jnp.concatenate(sides, axis=1).astype(BF16)
 
     def spread_z(i, c):
         to = lax.rem(z + i, NZ)
@@ -349,10 +384,9 @@
     lax.fori_loop(1, NZ, spread_z, 0)
     pltpu.make_async_copy(zsend.at[z], zrecv.at[z], z_r).start()
     drain(zrecv, z_r)
-    out = zrecv[0]
-    for j in range(1, NZ):
-        out = out + zrecv[j]
-    rg[...] = out[:, :R]
+    out = jnp.sum(zrecv[...].astype(F32), axis=0)
+    rg[:16] = out[:, :R]
+    rg[16:] = out[: ED - 16, 64 : 64 + R]
 
     for g in range(2):
         for st in range(RE):
@@ -372,7 +406,8 @@
         drain(w_rows(dp), wc_s.at[d])
         drain(tokg.at[dp], tc_s.at[d])
     drain(tokg.at[dp, pl.ds(0, NY - 1)], t1_s)
-    drain(lgb.at[pl.ds(0, NDP * NY - 1)], lg_s)
+    drain(erecv.at[pl.ds(0, NDP * NY - 1)], e_s)
+    drain(drecv.at[pl.ds(0, NDP * NY - 1)], d_s)
     drain(zsend.at[pl.ds(0, NZ - 1)], z_s)
 
 
@@ -393,15 +428,15 @@
     hid, lg, rg = pl.pallas_call(
         functools.partial(kernel, dims),
         out_shape=(
-            jax.ShapeDtypeStruct((NY, NZ * 8, FW), BF16),
-            jax.ShapeDtypeStruct((NDP, ED, T), F32),
-            jax.ShapeDtypeStruct((ED, R), F32),
+            pltpu.VMEM((NY, NZ * 8, FW), BF16),
+            pltpu.VMEM((NDP, ED, T), F32),
+            pltpu.VMEM((ED, R), F32),
         ),
-        in_specs=[vmem, vmem, vmem, hbm, hbm, hbm],
+        in_specs=[hbm] * 6,
         out_specs=(vmem, vmem, vmem),
         scratch_shapes=[
             pltpu.VMEM((2, RE, 2, T, H), BF16),
-            pltpu.VMEM((2 * RE + 1, 16, T), F32),
+            pltpu.VMEM((2 * RE + 1, 16, T), BF16),
             pltpu.VMEM((NN, NY, 16, H), BF16),
             pltpu.VMEM((NN, NY, 16, H), BF16),
             pltpu.VMEM((2, 2, RE * NY, 16, H // 2), BF16),
@@ -419,18 +454,23 @@
             pltpu.VMEM((NY, NZ, 8, FW), F32),
             pltpu.VMEM((NZ, NY, 1, 128), F32),
             pltpu.VMEM((NE, 1, 128), F32),
-            pltpu.VMEM((NDP * NY, ED, T), F32),
-            pltpu.VMEM((2 * ED, NDP * NY * T), BF16),
-            pltpu.VMEM((NZ, ED, 128), F32),
-            pltpu.VMEM((NZ, ED, 128), F32),
+            pltpu.VMEM((NDP, ED + 8, T), F32),
+            pltpu.VMEM((NDP * NY, ED + 8, T), F32),
+            pltpu.VMEM((8, T), F32),
+            pltpu.VMEM((NDP * NY, 8, T), F32),
+            pltpu.VMEM((NZ, 16, 128), BF16),
+            pltpu.VMEM((NZ, 16, 128), BF16),
             pltpu.VMEM((EX, T), F32),
             pltpu.VMEM((NE, T), F32),
             pltpu.VMEM((3, 8, T), F32),
+            pltpu.VMEM((T, D), BF16),
+            pltpu.VMEM((EX, T), F32),
+            pltpu.VMEM((8, T), jnp.int32),
             dma((2, RE, 2)), dma((2, RE, 2)), dma((2, RE)), dma((2, RE)),
             one, dma((NN,)), one, dma((NN,)), one, dma((2,)), one, one, one, one,
             dma((NX - 1,)), dma((NX - 1,)), dma((NX,)), dma((NX,)),
             one, one, dma((NX - 1,)), dma((NX - 1,)), dma((NX,)), dma((NX,)),
-            one, one, one, one, dma((2,)),
+            one, one, one, dma((NDP,)), one, one, dma((5,)),
         ],
         compiler_params=pltpu.CompilerParams(
             collective_id=0, has_side_effects=True, vmem_limit_bytes=58 * 2**20

time: 179 us -> 168 us (0.939)
  Pallas kernels: 174 us -> 165 us
    pallas_call x1, Pallas kernels: 174 us -> 165 us  [local(): pl.pallas_call(functools.partial(kernel, dims), out_shape=(pltpu.VMEM((NY...]
    unnamed x7 -> x3, local copies, waits for them, and re-layouts: 3.61 us -> 2.21 us
where the time goes in v3:
time: 168 us
  Pallas kernels  165 us (98%)
  local copies, waits for them, and re-layouts  2.21 us (1%)
    pallas_call x1, Pallas kernels, local(): pl.pallas_call(functools.partial(kernel, dims), out_shape=(pltpu.VMEM((NY...  165 us

profile of v3, /device:TPU:1, one launch (start us, length us, event | category | flops | bytes accessed | tf_op | source)
XLA Modules:
  0.0 168.3 jit_solution(16654646553831795154)
XLA Ops:
  0.6 165.4 %shard_map.85 = (bf16[4,128,1024]{2,1,0:T(8,128)(2,1)S(1)}, f32[8,24,128]{2,1,0:T(8,128)S(1)}, f32[24,56]{1,0:T(8,128)S(1)}) custom-call(bf16[128,3584]{1,0:T(8,128)(2,1)} %og_in.1, f32[192,128]{1,0:T(8,128)} %bitcast.14, s32[8,128]{1,0:T(8,128)} %bitcast.15, bf16[128,3584]{1,0:T(8,128)(2,1)} %tok.1, bf16[128,3584]{1,0:T(8,128)(2,1)} %bitcast.13, ...), custom_call_target="tpu_custom_call" | custom-call | flops 4000000000 | bytes 6000000 | tf_op jit(solution)/shard_map/pallas_call | solution.py:428
  166.1 1.0 copy.12
  167.0 0.6 copy.13
  167.7 0.6 copy.14

commit v4 on v3

--- a/solution.py
+++ b/solution.py
@@ -65,7 +65,8 @@
     barrier = pltpu.get_barrier_semaphore()
 
     def greet(i, c):
-        pl.semaphore_signal(barrier, inc=1, device_id=(dp, lax.rem(e + i, NE)), device_id_type=MESH)
+        away = jnp.where(i % 2 == 1, (i + 1) // 2, NE - i // 2)
+        pl.semaphore_signal(barrier, inc=1, device_id=(dp, lax.rem(e + away, NE)), device_id_type=MESH)
         return c
 
     lax.fori_loop(1, NE, greet, 0)
@@ -80,6 +81,109 @@
     load.start()
     own_w = pltpu.make_async_copy(w, wfull.at[pl.ds(pl.multiple_of(dp * FS, FS), FS)], local_sem.at[1])
     own_w.start()
+
+    lane8 = iota((NY, 8, 128), 2) == iota((NY, 8, 128), 1)
+
+    def slots(info):
+        info = info.astype(F32)
+        window = iota((NE, T), 0).astype(F32)
+        mask = jnp.zeros((NE, T), F32)
+        gate = jnp.zeros((NE, T), F32)
+        for k in range(8):
+            hit = window == info[k : k + 1, :]
+            mask = jnp.where(hit, 1.0, mask)
+            gate = jnp.where(hit, info[8 + k : 9 + k, :], gate)
+        earlier = (iota((T, T), 0) < iota((T, T), 1)).astype(F32).astype(BF16)
+        rank = jnp.dot(mask.astype(BF16), earlier, preferred_element_type=F32)
+        return jnp.where(mask > 0.0, rank, 255.0), gate
+
+    def tables(pos, gate, experts):
+        n = experts.shape[0]
+        pick = (iota((n, NE), 1) == experts).astype(F32).astype(BF16)
+        spread = jnp.dot(pick, pos.astype(BF16), preferred_element_type=F32)
+        hit = spread == (iota((n, T), 0) % 8).astype(F32)
+        gates_at = jnp.dot(pick, gate.astype(BF16), preferred_element_type=F32)
+        col = jnp.sum(jnp.where(hit, gates_at, 0.0), axis=1, keepdims=True).reshape(n // 8, 8, 1)
+        at = iota((n // 8, 8, 128), 2) == iota((n // 8, 8, 128), 1)
+        return hit.astype(F32).astype(BF16), jnp.sum(jnp.where(at, col, 0.0), axis=1, keepdims=True)
+
+    def dispatch(ni, low, high, pos, gate):
+        experts = iota((NY * 8, 1), 0) // 8 * NZ + z
+        table, rows = tables(pos, gate, experts)
+        gnsend[ni] = rows
+        a = jnp.dot(table, low, preferred_element_type=F32).reshape(NY, 8, H)
+        b = jnp.dot(table, high, preferred_element_type=F32).reshape(NY, 8, H)
+        nsend[ni] = jnp.concatenate([a, b], axis=1).astype(BF16)
+        for d in range(1, NY):
+            yy = lax.rem(y + d, NY)
+            remote(nsend.at[ni, yy], nrecv.at[ni, y], near_s, near_r.at[ni], (dp, yy * NZ + z)).start()
+            remote(gnsend.at[ni, yy], gnrecv.at[ni, y], gn_s, gn_r.at[ni], (dp, yy * NZ + z)).start()
+        pltpu.make_async_copy(nsend.at[ni, y], nrecv.at[ni, y], near_r.at[ni]).start()
+        pltpu.make_async_copy(gnsend.at[ni, y], gnrecv.at[ni, y], gn_r.at[ni]).start()
+
+    def hop_meta(g, st):
+        to = (dp, y * NZ + lax.rem(z + (1 if g == 0 else NZ - 1), NZ))
+        info = meta.at[2 * RE] if st == 0 else meta.at[g * RE + st - 1]
+        remote(info, meta.at[g * RE + st], meta_s.at[g, st], meta_r.at[g, st], to).start()
+
+    def hop(g, st, c):
+        to = (dp, y * NZ + lax.rem(z + (1 if g == 0 else NZ - 1), NZ))
+        src = og_in.at[:, pl.ds(c * H, H)] if st == 0 else ring.at[g, st - 1, c]
+        remote(src, ring.at[g, st, c], ring_s.at[g, st, c], ring_r.at[g, st, c], to).start()
+        if c == 0 and st > 0:
+            hop_meta(g, st)
+
+    def arrived(g, st, c):
+        if c == 0:
+            drain(meta.at[g * RE + st], meta_r.at[g, st])
+        drain(ring.at[g, st, c], ring_r.at[g, st, c])
+
+    def relay(g, c):
+        n = RE * NY
+        if c == 0:
+            d = iota((n * 8, 1), 0) // 8
+            step = d // NY + 1
+            experts = (y + d % NY) % NY * NZ + (z + (step if g == 0 else NZ - step)) % NZ
+            pos, gate = slots(meta[g * RE + RE - 1])
+            table, rows = tables(pos, gate, experts)
+            ftable[g] = table
+            gfsend[g] = rows
+        p = jnp.dot(ftable[g], ring[g, RE - 1, c], preferred_element_type=F32).reshape(n, 8, H)
+        fsend[c, g] = jnp.concatenate([p[:, :, : H // 2], p[:, :, H // 2 :]], axis=1).astype(BF16)
+
+        def one(d, carry):
+            j = d // NY + 1
+            to = (dp, lax.rem(y + d % NY, NY) * NZ + lax.rem(z + (j if g == 0 else NZ - j), NZ))
+            fi = j - 1 if g == 0 else jnp.where(j == RE, RE - 1, RE - 1 + j)
+            remote(fsend.at[c, g, d], frecv.at[c, fi, y], far_s, far_r.at[c], to).start()
+            if c == 0:
+                remote(gfsend.at[g, d], gfrecv.at[fi, y], gf_s, gf_r, to).start()
+            return carry
+
+        last = (RE - 1) * NY
+        split = last + NY // 2
+        lax.fori_loop(*((last, split) if g == 0 else (split, RE * NY)), one, 0)
+        lax.fori_loop(0, last, lambda i, carry: one(last - 1 - i, carry), 0)
+
+    def w_rows(owner):
+        return wfull.at[pl.ds(pl.multiple_of(owner * FS, FS), FS)]
+
+    def tok_cols(yy):
+        return tok.at[:, pl.ds(pl.multiple_of(yy * Q, 128), Q)]
+
+    pair = (x * NC + 1 - core, e)
+    pl.semaphore_wait(barrier, NE - 1 + (NDP - 1) * NY)
+
+    for c in range(2):
+        for g in range(2):
+            hop(g, 0, c)
+    for d in range(1, NX):
+        remote(w, w_rows(dp), wx_s.at[d - 1], wx_r.at[d - 1], (lax.rem(x + d, NX) * NC + core, e)).start()
+    remote(w, w_rows(dp), wc_s.at[0], wc_r.at[0], pair).start()
+    for d in range(1, NY):
+        yy = lax.rem(y + d, NY)
+        remote(tok_cols(yy), tokg.at[dp, y], t1_s, t1_r, (dp, yy * NZ + z)).start()
+    pltpu.make_async_copy(tok_cols(y), tokg.at[dp, y], t1_r).start()
 
     loads[0].wait()
     loads[1].wait()
@@ -107,106 +211,8 @@
         esend[d, :ED] = zterm[d * ED : (d + 1) * ED]
         esend[d, ED:] = names_f
     loads[2].wait()
-    lane8 = iota((NY, 8, 128), 2) == iota((NY, 8, 128), 1)
-
-    def slots(info):
-        info = info.astype(F32)
-        window = iota((NE, T), 0).astype(F32)
-        mask = jnp.zeros((NE, T), F32)
-        gate = jnp.zeros((NE, T), F32)
-        for k in range(8):
-            hit = window == info[k : k + 1, :]
-            mask = jnp.where(hit, 1.0, mask)
-            gate = jnp.where(hit, info[8 + k : 9 + k, :], gate)
-        earlier = (iota((T, T), 0) < iota((T, T), 1)).astype(F32).astype(BF16)
-        rank = jnp.dot(mask.astype(BF16), earlier, preferred_element_type=F32)
-        return jnp.where(mask > 0.0, rank, 255.0), gate
-
-    def tables(pos, gate, experts):
-        n = experts.shape[0]
-        pick = (iota((n, NE), 1) == experts).astype(F32).astype(BF16)
-        spread = jnp.dot(pick, pos.astype(BF16), preferred_element_type=F32)
-        hit = spread == (iota((n, T), 0) % 8).astype(F32)
-        gates_at = jnp.dot(pick, gate.astype(BF16), preferred_element_type=F32)
-        col = jnp.sum(jnp.where(hit, gates_at, 0.0), axis=1, keepdims=True).reshape(n // 8, 8, 1)
-        at = iota((n // 8, 8, 128), 2) == iota((n // 8, 8, 128), 1)
-        return hit.astype(F32).astype(BF16), jnp.sum(jnp.where(at, col, 0.0), axis=1, keepdims=True)
-
-    def dispatch(ni, low, high, pos, gate):
-        experts = iota((NY * 8, 1), 0) // 8 * NZ + z
-        table, rows = tables(pos, gate, experts)
-        gnsend[ni] = rows
-        a = jnp.dot(table, low, preferred_element_type=F32).reshape(NY, 8, H)
-        b = jnp.dot(table, high, preferred_element_type=F32).reshape(NY, 8, H)
-        nsend[ni] = jnp.concatenate([a, b], axis=1).astype(BF16)
-        for d in range(1, NY):
-            yy = lax.rem(y + d, NY)
-            remote(nsend.at[ni, yy], nrecv.at[ni, y], near_s, near_r.at[ni], (dp, yy * NZ + z)).start()
-            remote(gnsend.at[ni, yy], gnrecv.at[ni, y], gn_s, gn_r.at[ni], (dp, yy * NZ + z)).start()
-        pltpu.make_async_copy(nsend.at[ni, y], nrecv.at[ni, y], near_r.at[ni]).start()
-        pltpu.make_async_copy(gnsend.at[ni, y], gnrecv.at[ni, y], gn_r.at[ni]).start()
-
-    def hop(g, st, c):
-        to = (dp, y * NZ + lax.rem(z + (1 if g == 0 else NZ - 1), NZ))
-        src = og.at[:, pl.ds(c * H, H)] if st == 0 else ring.at[g, st - 1, c]
-        remote(src, ring.at[g, st, c], ring_s.at[g, st, c], ring_r.at[g, st, c], to).start()
-        if c == 0:
-            info = own_meta if st == 0 else meta.at[g * RE + st - 1]
-            remote(info, meta.at[g * RE + st], meta_s.at[g, st], meta_r.at[g, st], to).start()
-
-    def arrived(g, st, c):
-        if c == 0:
-            drain(meta.at[g * RE + st], meta_r.at[g, st])
-        drain(ring.at[g, st, c], ring_r.at[g, st, c])
-
-    def relay(g, c):
-        n = RE * NY
-        if c == 0:
-            d = iota((n * 8, 1), 0) // 8
-            step = d // NY + 1
-            experts = (y + d % NY) % NY * NZ + (z + (step if g == 0 else NZ - step)) % NZ
-            pos, gate = slots(meta[g * RE + RE - 1])
-            table, rows = tables(pos, gate, experts)
-            ftable[g] = table
-            gfsend[g] = rows
-        p = jnp.dot(ftable[g], ring[g, RE - 1, c], preferred_element_type=F32).reshape(n, 8, H)
-        fsend[c, g] = jnp.concatenate([p[:, :, : H // 2], p[:, :, H // 2 :]], axis=1).astype(BF16)
-
-        def one(d, carry):
-            j = d // NY + 1
-            to = (dp, lax.rem(y + d % NY, NY) * NZ + lax.rem(z + (j if g == 0 else NZ - j), NZ))
-            fi = j - 1 if g == 0 else jnp.where(j == RE, RE - 1, RE - 1 + j)
-            remote(fsend.at[c, g, d], frecv.at[c, fi, y], far_s, far_r.at[c], to).start()
-            if c == 0:
-                remote(gfsend.at[g, d], gfrecv.at[fi, y], gf_s, gf_r, to).start()
-            return carry
-
-        last = (RE - 1) * NY
-        split = last + NY // 2
-        lax.fori_loop(*((last, split) if g == 0 else (split, RE * NY)), one, 0)
-        lax.fori_loop(0, last, lambda i, carry: one(last - 1 - i, carry), 0)
-
-    def w_rows(owner):
-        return wfull.at[pl.ds(pl.multiple_of(owner * FS, FS), FS)]
-
-    def tok_cols(yy):
-        return tok.at[:, pl.ds(pl.multiple_of(yy * Q, 128), Q)]
-
-    pair = (x * NC + 1 - core, e)
-    own_w.wait()
-    pl.semaphore_wait(barrier, NE - 1 + (NDP - 1) * NY)
-
-    for c in range(2):
-        for g in range(2):
-            hop(g, 0, c)
-    for d in range(1, NX):
-        remote(w_rows(dp), w_rows(dp), wx_s.at[d - 1], wx_r.at[d - 1], (lax.rem(x + d, NX) * NC + core, e)).start()
-    remote(w_rows(dp), w_rows(dp), wc_s.at[0], wc_r.at[0], pair).start()
-    for d in range(1, NY):
-        yy = lax.rem(y + d, NY)
-        remote(tok_cols(yy), tokg.at[dp, y], t1_s, t1_r, (dp, yy * NZ + z)).start()
-    pltpu.make_async_copy(tok_cols(y), tokg.at[dp, y], t1_r).start()
-
+    for g in range(2):
+        hop_meta(g, 0)
     mine = dp * NY + y
 
     def spread_early(i, c):
@@ -292,6 +298,7 @@
     for d in range(NX):
         shard = lax.rem(x + NX - d, NX) * NC + 1 - core
         drain(w_rows(shard), wc_r.at[d])
+    own_w.wait()
     near([0, 1, 2])
     for first in range(3, NN, 4):
         near(list(range(first, min(first + 4, NN))))
@@ -353,7 +360,7 @@
     own_names = (iota((ED, T), 0) + dp * ED).astype(F32)
     panel = jnp.zeros((2 * ED, Q), F32)
     for i in range(NDP):
-        owner = lax.rem(dp + i, NDP)
+        owner = lax.rem(dp + NDP - i, NDP)
         drain(drecv.at[pl.ds(owner * NY, NY)], d_r.at[owner])
         parts = []
         for yy in range(NY):

time: 168 us -> 170 us (1.012)
  Pallas kernels: 165 us -> 167 us
    pallas_call x1, Pallas kernels: 165 us -> 167 us  [local(): pl.pallas_call(functools.partial(kernel, dims), out_shape=(pltpu.VMEM((NY...]
where the time goes in v4:
time: 170 us
  Pallas kernels  167 us (98%)
  local copies, waits for them, and re-layouts  2.21 us (1%)
    pallas_call x1, Pallas kernels, local(): pl.pallas_call(functools.partial(kernel, dims), out_shape=(pltpu.VMEM((NY...  167 us

profile of v4, /device:TPU:1, one launch (start us, length us, event | category | flops | bytes accessed | tf_op | source)
XLA Modules:
  0.0 170.1 jit_solution(10233348567868537223)
XLA Ops:
  0.6 167.3 %shard_map.85 = (bf16[4,128,1024]{2,1,0:T(8,128)(2,1)S(1)}, f32[8,24,128]{2,1,0:T(8,128)S(1)}, f32[24,56]{1,0:T(8,128)S(1)}) custom-call(bf16[128,3584]{1,0:T(8,128)(2,1)} %og_in.1, f32[192,128]{1,0:T(8,128)} %bitcast.14, s32[8,128]{1,0:T(8,128)} %bitcast.15, bf16[128,3584]{1,0:T(8,128)(2,1)} %tok.1, bf16[128,3584]{1,0:T(8,128)(2,1)} %bitcast.13, ...), custom_call_target="tpu_custom_call" | custom-call | flops 4000000000 | bytes 6000000 | tf_op jit(solution)/shard_map/pallas_call | solution.py:435
  167.9 1.0 copy.12
  168.9 0.6 copy.13
  169.5 0.6 copy.14

commit v5 on v3

--- a/solution.py
+++ b/solution.py
@@ -313,7 +313,7 @@
     for f in range(0, FW, FC):
         g = lax.dot_general(rows, wfull[f : f + FC, H:], nt, preferred_element_type=F32)
         finish(f, g + half[:, f : f + FC], backs, columns, sources)
-    for i in range(NF):
+    for i in sorted(range(NF), key=lambda i: -(RE + 1 + i if i < RE else NZ - 1 - i)):
         give_back(NN + i, sources[i], backs[i])
     hid[...] = hidf[...].reshape(NY, NZ * 8, FW).astype(BF16)
     for d in range(NX):
@@ -337,11 +337,13 @@
     dsend[...] = dchosen
 
     def spread_d(i, c):
+        i = lax.rem(i + NDP * NY // 2, NDP * NY)
         to_dp, to_y = lax.rem(dp + i // NY, NDP), lax.rem(y + i, NY)
         remote(dsend, drecv.at[mine], d_s, d_r.at[dp], (to_dp, to_y * NZ + z)).start()
         return c
 
-    lax.fori_loop(1, NDP * NY, spread_d, 0)
+    lax.fori_loop(0, NDP * NY // 2, spread_d, 0)
+    lax.fori_loop(NDP * NY // 2 + 1, NDP * NY, spread_d, 0)
     pltpu.make_async_copy(dsend, drecv.at[mine], d_r.at[dp]).start()
     names = iota((EX, T), 0)
     lgt = zterm[...]
@@ -377,11 +379,12 @@
         zsend[j] = jnp.concatenate(sides, axis=1).astype(BF16)
 
     def spread_z(i, c):
-        to = lax.rem(z + i, NZ)
+        step = (i + 1) // 2
+        to = lax.rem(z + NZ // 2 + jnp.where(i % 2 == 1, NZ - step, step), NZ)
         remote(zsend.at[to], zrecv.at[z], z_s, z_r, (dp, y * NZ + to)).start()
         return c
 
-    lax.fori_loop(1, NZ, spread_z, 0)
+    lax.fori_loop(0, NZ - 1, spread_z, 0)
     pltpu.make_async_copy(zsend.at[z], zrecv.at[z], z_r).start()
     drain(zrecv, z_r)
     out = jnp.sum(zrecv[...].astype(F32), axis=0)

time: 168 us -> 168 us (level)
  no operation moved by 1% of the time
where the time goes in v5:
time: 168 us
  Pallas kernels  165 us (98%)
  local copies, waits for them, and re-layouts  2.21 us (1%)
    pallas_call x1, Pallas kernels, local(): pl.pallas_call(functools.partial(kernel, dims), out_shape=(pltpu.VMEM((NY...  165 us

profile of v5, /device:TPU:1, one launch (start us, length us, event | category | flops | bytes accessed | tf_op | source)
XLA Modules:
  0.0 167.6 jit_solution(10235180089323617194)
XLA Ops:
  0.6 164.7 %shard_map.85 = (bf16[4,128,1024]{2,1,0:T(8,128)(2,1)S(1)}, f32[8,24,128]{2,1,0:T(8,128)S(1)}, f32[24,56]{1,0:T(8,128)S(1)}) custom-call(bf16[128,3584]{1,0:T(8,128)(2,1)} %og_in.1, f32[192,128]{1,0:T(8,128)} %bitcast.14, s32[8,128]{1,0:T(8,128)} %bitcast.15, bf16[128,3584]{1,0:T(8,128)(2,1)} %tok.1, bf16[128,3584]{1,0:T(8,128)(2,1)} %bitcast.13, ...), custom_call_target="tpu_custom_call" | custom-call | flops 4000000000 | bytes 6000000 | tf_op jit(solution)/shard_map/pallas_call | solution.py:431
  165.4 1.0 copy.12
  166.3 0.6 copy.13
  167.0 0.6 copy.14
